TPU v7x, 768 devices: a whole 4x8x12 slice. The times are simulated.
768 devices in a mesh: seq: 192 (over z, x, y_lo), head: 4 (over y_hi, core).
Axes of the slice: x: 4, y: 8 (y_hi: 2, y_lo: 4; y = y_hi * 4 + y_lo), z: 12, core: 2. Of those that a mesh axis runs over, the one named last changes fastest.
Arguments:
- tokens: bfloat16 [98304, 2048], P('seq', 'head')
- w_query: bfloat16 [2048, 2048], P(None, 'head'), may hold values from -0.125 to 0.125
- w_key: bfloat16 [2048, 2048], P(None, 'head'), may hold values from -0.125 to 0.125
- w_value: bfloat16 [2048, 2048], P(None, 'head'), may hold values from -0.125 to 0.125
- window: int32 [768], replicated, may hold values from 0 to 4, as said below
- global_blocks: int32 [768, 2], replicated, may hold values from 0 to 767, as said below
- file_bounds: int32 [2, 98304], replicated, may hold values from 0 to 98304, as said below
Outputs:
- attended: bfloat16 [98304, 2048], P('seq', 'head')
Inputs may be any that keep to these rules, and one draw needn't show every extreme that they name: `window`: blocks fall into aligned runs of 4; in each aligned pair of runs one run has half-widths of 1 or more with one exactly 4, and the other run has all half-widths 0. `global_blocks`: every listed global block lies at most 4 blocks before or after its query block, and some lie exactly 4 away; a listed block may lie outside the query's file; in a run whose half-widths are all 0 the listed blocks lie in that run. `file_bounds`: files are runs of whole tokens holding the token itself; no file crosses a position k * 2048 - 2048 // 2, each file has at most 2048 tokens, and one file has exactly 2048.
All inputs are finite; a program needn't handle non-finite values.
Results may differ from a plain program's by a relative error of at most 0.012.
The roundings to bfloat16 on the way count: a program that leaves them out, or rounds other values in their place, can miss the bound.
Values may be sent and summed in bfloat16 or wider, within the bound.
A program may use at most 128 MiB of HBM per device.

v0:
```python
import jax
import jax.numpy as jnp
from jax import lax
from jax.sharding import PartitionSpec as P

HEAD_DIM = 128
BLOCK = 128


def extended_2(shard, sides, width):
    for axis, dim in sides:
        size, length = (lax.axis_size(axis), shard.shape[dim])
        up = [(i, (i + 1) % size) for i in range(size - 1)]
        down = [(j, i) for i, j in up]
        last = lax.slice_in_dim(shard, length - width, length, axis=dim)
        leading = lax.slice_in_dim(shard, 0, width, axis=dim)
        before = lax.ppermute(last, axis, up)
        after = lax.ppermute(leading, axis, down)
        shard = jnp.concatenate([before, shard, after], axis=dim)
    return shard


def project(rows, weight):
    return jnp.dot(rows, weight, preferred_element_type=jnp.float32).astype(jnp.bfloat16)


def attend(rows_q, q_first, keys, values, k_first, window, global_blocks, file_bounds):
    count = rows_q.shape[0]
    span = keys.shape[0]
    features = rows_q.shape[1]
    heads_dev = features // HEAD_DIM
    q_pos = q_first + jnp.arange(count, dtype=jnp.int32)
    q_blk = jnp.floor_divide(q_pos, BLOCK)
    key_pos = k_first + jnp.arange(span, dtype=jnp.int32)
    key_blk = jnp.floor_divide(key_pos, BLOCK)
    row_window = jnp.take(window, q_blk)
    row_global = jnp.take(global_blocks, q_blk, axis=0)
    starts = lax.dynamic_slice(file_bounds[0], (q_first,), (count,))
    ends = lax.dynamic_slice(file_bounds[1], (q_first,), (count,))
    near = jnp.abs(q_blk[:, None] - key_blk[None, :]) <= row_window[:, None]
    listed = jnp.any(row_global[:, :, None] == key_blk[None, None, :], axis=1)
    infile = (key_pos[None, :] >= starts[:, None]) & (key_pos[None, :] < ends[:, None])
    allowed = infile & (near | listed)
    query3 = rows_q.reshape(count, heads_dev, HEAD_DIM)
    keys3 = keys.reshape(span, heads_dev, HEAD_DIM)
    values3 = values.reshape(span, heads_dev, HEAD_DIM)
    score = jnp.einsum(
        "qhd,khd->hqk", query3, keys3, preferred_element_type=jnp.float32
    ) * HEAD_DIM ** (-0.5)
    score = jnp.where(allowed[None], score, -jnp.inf)
    top = jnp.max(score, axis=2, keepdims=True)
    expo = jnp.exp(score - top)
    weight = (expo / jnp.sum(expo, axis=2, keepdims=True)).astype(jnp.bfloat16)
    mixed = jnp.einsum("hqk,khd->qhd", weight, values3, preferred_element_type=jnp.float32)
    return mixed.astype(jnp.bfloat16).reshape(count, features)


def wide_run(run, blk_dev, window, global_blocks):
    first = run * blk_dev
    widths = lax.dynamic_slice(window, (first,), (blk_dev,))
    listed = lax.dynamic_slice(
        global_blocks, (first, jnp.zeros((), jnp.int32)), (blk_dev, global_blocks.shape[1])
    )
    outside = (listed < first) | (listed >= first + blk_dev)
    return jnp.any(widths > 0) | jnp.any(outside)


def local(tokens, w_query, w_key, w_value, window, global_blocks, file_bounds):
    tok_rows = tokens.shape[0]
    blk_dev = tok_rows // BLOCK
    device = lax.axis_index("seq")
    whole = lax.all_gather(tokens, "head", axis=1, tiled=True)
    query = project(whole, w_query)
    paired = jnp.stack([project(whole, w_key), project(whole, w_value)])
    extended = extended_2(paired, (("seq", 1),), tok_rows)
    keys = extended[0]
    values = extended[1]
    own_first = device * tok_rows
    ext_first = own_first - tok_rows
    me_wide = wide_run(device, blk_dev, window, global_blocks)

    def narrow_rows(rows_q, q_first):
        return attend(
            rows_q,
            q_first,
            keys[tok_rows : 2 * tok_rows],
            values[tok_rows : 2 * tok_rows],
            own_first,
            window,
            global_blocks,
            file_bounds,
        )

    def full_rows(rows_q, q_first):
        return attend(rows_q, q_first, keys, values, ext_first, window, global_blocks, file_bounds)

    attended = lax.cond(
        me_wide, lambda: full_rows(query, own_first), lambda: narrow_rows(query, own_first)
    )
    return attended


def solution(mesh):
    placed = (P("seq", "head"), P(None, "head"), P(None, "head"), P(None, "head"), P(), P(), P())
    return jax.shard_map(
        local, mesh=mesh, in_specs=placed, out_specs=P("seq", "head"), check_vma=False
    )
```

profile of v0, /device:TPU:25, one launch (start us, length us, event | category | flops | bytes accessed | tf_op | source)
XLA Modules:
  0.0 174.1 jit_solution(15883710629755083369)
XLA Ops:
  6.5 0.0 copy-start
  6.5 0.0 all-gather.2.cloned.1.call-start
  6.5 0.7 all-gather.2.cloned.1.call-update
  7.3 52.2 %all-gather.2.cloned.1.call-done = bf16[512,2048]{1,0:T(8,128)(2,1)} async-done(((bf16[512,512]{1,0:T(8,128)(2,1)}), bf16[512,2048]{1,0:T(8,128)(2,1)}) %all-gather.2.cloned.1.call-update) | async-done | bytes 2097168 | tf_op jit(solution)/shard_map/all_gather | solution.py:72
  59.5 0.0 copy-done
  59.5 0.0 copy-start.12
  59.5 0.0 copy-start.13
  59.5 3.0 %fusion.48 = bf16[1,512,512]{2,1,0:T(8,128)(2,1)S(1)} fusion(bf16[512,2048]{1,0:T(8,128)(2,1)} %all-gather.2.cloned.1.call-done, bf16[2048,512]{1,0:T(8,128)(2,1)S(1)} %copy-done), kind=kOutput, calls=%fused_computation.91 | convolution fusion | flops 1074003968 | bytes 4718592 | tf_op jit(solution)/shard_map/dot_general | solution.py:24
  62.5 0.0 copy-done.12
  62.5 0.0 copy-done.13
  62.5 0.0 copy-start.3
  62.5 0.0 copy-start.1
  62.5 0.0 copy-start.10
  62.5 1.2 fusion.47
  63.8 0.0 copy-done.3
  63.8 0.0 copy-start.5
  63.8 1.1 pad_maximum_fusion.1
  64.9 0.0 copy-done.5
  64.9 5.7 %collective-permute-start.1 = (bf16[2,512,512]{2,1,0:T(8,128)(2,1)}, bf16[2,512,512]{2,1,0:T(8,128)(2,1)}, u32[]{:S(2)}, u32[]{:S(2)}) collective-permute-start(bf16[2,512,512]{2,1,0:T(8,128)(2,1)} %pad_maximum_fusion.1), channel_id=1, source_target_pairs={{4,0},{8,4},{12,8},{16,12},{20,16},{24,20},{28,24},{32,28},{36,32}... | collective-permute-start | bytes 3145736 | tf_op jit(solution)/shard_map/ppermute | solution.py:18
  70.6 4.9 %collective-permute-start = (bf16[2,512,512]{2,1,0:T(8,128)(2,1)}, bf16[2,512,512]{2,1,0:T(8,128)(2,1)}, u32[]{:S(2)}, u32[]{:S(2)}) collective-permute-start(bf16[2,512,512]{2,1,0:T(8,128)(2,1)} %pad_maximum_fusion.1), channel_id=1, source_target_pairs={{0,4},{4,8},{8,12},{12,16},{16,20},{20,24},{24,28},{28,32},{32,36}... | collective-permute-start | bytes 3145736 | tf_op jit(solution)/shard_map/ppermute | solution.py:17
  75.6 0.0 copy-done.1
  75.6 0.7 compare_reduce_fusion.2
  76.3 0.0 copy-done.10
  76.3 0.7 or_reduce_fusion
  78.2 0.0 copy-start.4
  78.2 0.0 copy-start.6
  78.2 4.3 %convolution_convert_fusion.2 = bf16[512,512]{1,0:T(8,128)(2,1)} fusion(bf16[512,2048]{1,0:T(8,128)(2,1)} %all-gather.2.cloned.1.call-done, bf16[2048,512]{1,0:T(8,128)(2,1)} %param.14), kind=kOutput, calls=%fused_computation.89 | convolution fusion | flops 1074003968 | bytes 4718592 | tf_op jit(solution)/shard_map/dot_general | solution.py:24
  82.5 0.0 copy-start.2
  82.5 14.8 %collective-permute-done.1 = bf16[2,512,512]{2,1,0:T(8,128)(2,1)} collective-permute-done((bf16[2,512,512]{2,1,0:T(8,128)(2,1)}, bf16[2,512,512]{2,1,0:T(8,128)(2,1)}, u32[]{:S(2)}, u32[]{:S(2)}) %collective-permute-start.1) | collective-permute-done | bytes 1048608 | tf_op jit(solution)/shard_map/ppermute | solution.py:18
  97.3 22.9 %collective-permute-done = bf16[2,512,512]{2,1,0:T(8,128)(2,1)} collective-permute-done((bf16[2,512,512]{2,1,0:T(8,128)(2,1)}, bf16[2,512,512]{2,1,0:T(8,128)(2,1)}, u32[]{:S(2)}, u32[]{:S(2)}) %collective-permute-start) | collective-permute-done | bytes 1048608 | tf_op jit(solution)/shard_map/ppermute | solution.py:17
  120.2 0.0 copy-done.4
  120.2 0.0 copy-done.6
  120.2 3.0 %pad_maximum_fusion = bf16[2,1536,512]{2,1,0:T(8,128)(2,1)} fusion(bf16[2,512,512]{2,1,0:T(8,128)(2,1)} %collective-permute-done.1, bf16[1,512,512]{2,1,0:T(8,128)(2,1)S(1)} %copy-done.4, bf16[1,512,512]{2,1,0:T(8,128)(2,1)S(1)} %copy-done.6, bf16[2,512,512]{2,1,0:T(8,128)(2,1)} %collective-permute-done), kind=kLoop, calls=%fused_computation.86 | loop fusion | flops 12582912 | bytes 6291456 | tf_op jit(solution)/shard_map/concatenate | solution.py:19
  123.2 0.0 copy-done.2
  123.2 43.2 %conditional.1 = (bf16[512,512]{1,0:T(8,128)(2,1)S(1)}) conditional(s32[]{:T(128)} %convert_element_type.32, (s32[]{:T(128)}, s32[2,98304]{1,0:T(2,128)S(1)}, s32[768]{0:T(1024)S(1)}, s32[768,2]{0,1:T(2,128)S(1)}, bf16[512,512]{1,0:T(8,128)(2,1)}, /*index=5*/bf16[2,1536,512]{2,1,0:T(8,128)(2,1)}, ...), branch_computations={%region_2.8_spmd.clone, %region_6.12_spmd.clone} | conditional | flops 1638460928 | bytes 56235152 | solution.py:97
  123.2 0.5 compare_and_fusion.1
  123.8 0.6 compare_select_fusion.1
  124.4 2.3 %gather_fusion.2 = s32[512]{0:T(512)S(1)} fusion(s32[768]{0:T(1024)S(1)} %get-tuple-element.100, s32[1024]{0:T(1024)S(1)} %pad_clamp_fusion.1), kind=kCustom, calls=%fused_computation.2.clone | custom fusion | bytes 6144 | tf_op jit(solution)/shard_map/cond/branch_1_fun/jit(_take)/gather | solution.py:36
  126.7 0.6 broadcast_select_fusion.3
  127.3 0.6 add_select_fusion.1
  127.8 0.2 copy.59
  128.0 1.0 gather_fusion.3
  129.1 0.0 copy-start.11
  129.1 0.8 broadcast_select_fusion.2
  129.9 0.1 copy.53
  130.0 0.6 compare_reduce_fusion.1
  130.6 0.6 fusion.51
  131.2 0.0 copy-done.11
  131.2 2.8 %fusion.24 = pred[512,1536]{1,0:T(8,128)(4,1)S(1)} fusion(pred[512,1536]{1,0:T(8,128)(4,1)S(1)} %compare_reduce_fusion.1, s32[512]{0:T(512)S(1)} %copy-done.11, s32[1536]{0:T(1024)S(1)} %get-tuple-element.185, s32[512]{0:T(512)} %get-tuple-element.184, s32[1536]{0:T(1024)} %get-tuple-element.186, s32[512]{0:T(512)S(1)} %bitcast.63, s32[512]{0:T(512)S(1)} %bitcast.64), kind=kLoop, calls=%fused_computation.51 | loop fusion | flops 6291456 | bytes 1593344 | tf_op jit(solution)/shard_map/cond/branch_1_fun/and | solution.py:43
  134.0 4.6 %copy.61 = bf16[2,1536,512]{1,2,0:T(8,128)(2,1)} copy(bf16[2,1536,512]{2,1,0:T(8,128)(2,1)} %get-tuple-element.169) | data formatting | bytes 6291456 | tf_op jit(solution)/shard_map
  138.7 2.6 %slice.57 = bf16[1,1536,512]{1,2,0:T(8,128)(2,1)} slice(bf16[2,1536,512]{1,2,0:T(8,128)(2,1)} %copy.61), slice={[1:2], [0:1536], [0:512]} | slice | bytes 3145728 | tf_op jit(solution)/shard_map/slice | solution.py:77
  141.3 4.6 %copy.60 = bf16[2,1536,512]{1,2,0:T(8,128)(2,1)} copy(bf16[2,1536,512]{2,1,0:T(8,128)(2,1)} %get-tuple-element.169) | data formatting | bytes 6291456 | tf_op jit(solution)/shard_map
  146.0 0.0 copy-start.8
  146.0 2.8 %slice.56 = bf16[1,1536,512]{1,2,0:T(8,128)(2,1)} slice(bf16[2,1536,512]{1,2,0:T(8,128)(2,1)} %copy.60), slice={[0:1], [0:1536], [0:512]} | slice | bytes 3145728 | tf_op jit(solution)/shard_map/slice | solution.py:76
  148.7 0.0 copy-done.8
  148.7 10.2 %fusion.52 = (f32[4,512]{1,0:T(4,128)S(1)}, f32[4,512,1536]{2,1,0:T(8,128)}) fusion(pred[512,1536]{1,0:T(8,128)(4,1)S(1)} %fusion.24, bf16[1536,4,128]{0,2,1:T(8,128)(2,1)} %bitcast.59, bf16[512,512]{1,0:T(8,128)(2,1)S(1)} %copy-done.8), kind=kOutput, calls=%fused_computation.98 | convolution fusion | flops 817890816 | bytes 15474688 | tf_op jit(solution)/shard_map/cond/branch_1_fun/sub | solution.py:52
  158.9 7.3 %fusion.27 = bf16[4,512,128]{1,2,0:T(8,128)(2,1)S(1)} fusion(bf16[1536,4,128]{0,2,1:T(8,128)(2,1)} %bitcast.58, f32[4,512,1536]{2,1,0:T(8,128)} %get-tuple-element.182, f32[4,512]{1,0:T(4,128)S(1)} %get-tuple-element.181), kind=kOutput, calls=%fused_computation.53 | convolution fusion | flops 811859968 | bytes 14688256 | tf_op jit(solution)/shard_map/cond/branch_1_fun/hqk,khd->qhd/dot_general | solution.py:54
  166.2 0.2 copy.67
  166.4 0.0 copy-start.9
  166.4 0.8 copy-done.9
  (2 shorter events, 0.0 us)
Async XLA Ops:
  6.5 52.9 %copy-start = (bf16[2048,512]{1,0:T(8,128)(2,1)S(1)}, bf16[2048,512]{1,0:T(8,128)(2,1)}, u32[]{:S(2)}) copy-start(bf16[2048,512]{1,0:T(8,128)(2,1)} %param.16) | copy-start | bytes 6291460
  6.5 52.9 %all-gather.2.cloned.1.call-start = ((), (), s32[]{:S(2)}) async-start(), calls=%async_computation | async-start | bytes 2621440 | tf_op jit(solution)/shard_map/all_gather | solution.py:72
  59.5 3.0 %copy-start.12 = (bf16[2048,512]{1,0:T(8,128)(2,1)S(1)}, bf16[2048,512]{1,0:T(8,128)(2,1)}, u32[]{:S(2)}) copy-start(bf16[2048,512]{1,0:T(8,128)(2,1)} %param.15) | copy-start | bytes 6291460
  59.5 3.0 %copy-start.13 = (bf16[512,2048]{1,0:T(8,128)(2,1)S(1)}, bf16[512,2048]{1,0:T(8,128)(2,1)}, u32[]{:S(2)}) copy-start(bf16[512,2048]{1,0:T(8,128)(2,1)} %all-gather.2.cloned.1.call-done) | copy-start | bytes 6291460
  62.5 1.3 copy-start.3
  62.5 13.1 %copy-start.1 = (s32[768]{0:T(1024)S(1)}, s32[768]{0:T(1024)}, u32[]{:S(2)}) copy-start(s32[768]{0:T(1024)} %param.17) | copy-start | bytes 9220
  62.5 13.8 %copy-start.10 = (s32[768,2]{0,1:T(2,128)S(1)}, s32[768,2]{0,1:T(2,128)}, u32[]{:S(2)}) copy-start(s32[768,2]{0,1:T(2,128)} %param.18) | copy-start | bytes 18436
  63.8 1.1 copy-start.5
  64.9 32.4 %collective-permute-start.1 = (bf16[2,512,512]{2,1,0:T(8,128)(2,1)}, bf16[2,512,512]{2,1,0:T(8,128)(2,1)}, u32[]{:S(2)}, u32[]{:S(2)}) collective-permute-start(bf16[2,512,512]{2,1,0:T(8,128)(2,1)} %pad_maximum_fusion.1), channel_id=1, source_target_pairs={{4,0},{8,4},{12,8},{16,12},{20,16},{24,20},{28,24},{32,28},{36,32}... | collective-permute-start | bytes 3145736 | tf_op jit(solution)/shard_map/ppermute | solution.py:18
  70.6 49.6 %collective-permute-start = (bf16[2,512,512]{2,1,0:T(8,128)(2,1)}, bf16[2,512,512]{2,1,0:T(8,128)(2,1)}, u32[]{:S(2)}, u32[]{:S(2)}) collective-permute-start(bf16[2,512,512]{2,1,0:T(8,128)(2,1)} %pad_maximum_fusion.1), channel_id=1, source_target_pairs={{0,4},{4,8},{8,12},{12,16},{16,20},{20,24},{24,28},{28,32},{32,36}... | collective-permute-start | bytes 3145736 | tf_op jit(solution)/shard_map/ppermute | solution.py:17
  78.2 42.0 %copy-start.4 = (bf16[1,512,512]{2,1,0:T(8,128)(2,1)S(1)}, bf16[1,512,512]{2,1,0:T(8,128)(2,1)}, u32[]{:S(2)}) copy-start(bf16[1,512,512]{2,1,0:T(8,128)(2,1)} %copy-done.3) | copy-start | bytes 1572868
  78.2 42.0 %copy-start.6 = (bf16[1,512,512]{2,1,0:T(8,128)(2,1)S(1)}, bf16[1,512,512]{2,1,0:T(8,128)(2,1)}, u32[]{:S(2)}) copy-start(bf16[1,512,512]{2,1,0:T(8,128)(2,1)} %copy-done.5) | copy-start | bytes 1572868
  82.5 40.7 %copy-start.2 = (s32[2,98304]{1,0:T(2,128)S(1)}, s32[2,98304]{1,0:T(2,128)}, u32[]{:S(2)}) copy-start(s32[2,98304]{1,0:T(2,128)} %param.19) | copy-start | bytes 2359300
  129.1 2.1 %copy-start.11 = (s32[512]{0:T(512)S(1)}, s32[512]{0:T(512)}, u32[]{:S(2)}) copy-start(s32[512]{0:T(512)} %broadcast_select_fusion.3) | copy-start | bytes 6148 | tf_op jit(solution)/shard_map/cond
  146.0 2.8 %copy-start.8 = (bf16[512,512]{1,0:T(8,128)(2,1)S(1)}, bf16[512,512]{1,0:T(8,128)(2,1)}, u32[]{:S(2)}) copy-start(bf16[512,512]{1,0:T(8,128)(2,1)} %get-tuple-element.102) | copy-start | bytes 1572868 | tf_op jit(solution)/shard_map/cond
  166.4 0.8 copy-start.9
Sparse Core Ops, SparseCore 0:
  9.8 49.6 all-gather.1
where the time goes:
time: 175 us; the launch traced here: 174 us
  waiting for transfers between devices  90.6 us (52%)
  matrix products  26.1 us (15%)
  local copies, waits for them, and re-layouts  20 us (11%)
  between operations  14.7 us (8%)
  other arithmetic  12 us (7%)
  starting transfers between devices  10.6 us (6%)
    all_gather x1, waiting for transfers between devices, local(): whole = lax.all_gather(tokens, 'head', axis=1, tiled=True)  52.2 us
    ppermute x1, waiting for transfers between devices, extended_2(): before = lax.ppermute(last, axis, up)  22.9 us
    ppermute x1, waiting for transfers between devices, extended_2(): after = lax.ppermute(leading, axis, down)  14.8 us
    sub x1, matrix products, attend(): expo = jnp.exp(score - top)  10.2 us
    another operation x3, local copies, waits for them, and re-layouts  9.46 us
    dot_general x3, matrix products, project(): jnp.dot(rows, weight, preferred_element_type=jnp.float32)  8.58 us
    dot_general x1, matrix products, attend(): jnp.einsum('hqk,khd->qhd', weight, values3, preferred_element_type=jnp.fl...  7.27 us
    ppermute x1, starting transfers between devices, extended_2(): after = lax.ppermute(leading, axis, down)  5.69 us
  transfers between devices with their start and end apart: 3, of which 3 were waited for; matrix products, arithmetic and copies ran while one was open for 3% of the time, Pallas kernels for 0%

commit v1 on v0

v1 whole, which is shorter than its diff:
```python
import functools

import jax
import jax.numpy as jnp
from jax import lax
from jax.experimental import pallas as pl
from jax.experimental.pallas import tpu as pltpu
from jax.sharding import PartitionSpec as P

MESH = pl.DeviceIdType.MESH
HEAD_DIM = 128
BLOCK = 128
ROWS = 512
FEAT = 512
HALF = 256
RING = 8
HEADS = 4
SUBS = 4
SUB = HALF // SUBS
BND = 8
OTHER = 10
LONG = 5


def kernel(groups, tok, wq, wk, wv, win, glob, fb, out, big, wbuf, qbuf, kvbuf, bias, bounds,
           acc, top, total, ring_sem, side_sem, recv_sem, local_sem):
    seq = lax.axis_index("seq")
    head = lax.axis_index("head")
    group = seq // 4
    low = seq % 4
    half_id = head // 2
    core = head % 2
    y = half_id * 4 + low
    odd = low % 2
    sgn = 1 - 2 * odd

    def at(g, yy, c):
        yy = lax.rem(yy + 2 * RING, RING)
        return (g * 4 + lax.rem(yy, 4), (yy // 4) * 2 + c)

    def slot_of(yy):
        return lax.rem(yy + 2 * RING, RING)

    up, down = at(group, y + 1, core), at(group, y - 1, core)
    mate = at(group, y, 1 - core)
    side_to = at(lax.rem(group + sgn + groups, groups), y, core)
    side_from = at(lax.rem(group - sgn + groups, groups), y, core)

    own_first = pl.multiple_of(seq * ROWS, ROWS)
    loads = [
        pltpu.make_async_copy(tok, big.at[y], local_sem.at[0]),
        pltpu.make_async_copy(fb.at[:, pl.ds(own_first, ROWS)], bounds, local_sem.at[1]),
        pltpu.make_async_copy(wq, wbuf.at[:, pl.ds(0, 512)], local_sem.at[2]),
        pltpu.make_async_copy(wk, wbuf.at[:, pl.ds(512, 512)], local_sem.at[3]),
        pltpu.make_async_copy(wv, wbuf.at[:, pl.ds(1024, 512)], local_sem.at[4]),
    ]
    for load in loads:
        load.start()

    barrier = pltpu.get_barrier_semaphore()
    for peer in (up, down, mate, side_to, side_from):
        pl.semaphore_signal(barrier, inc=1, device_id=peer, device_id_type=MESH)
    pl.semaphore_wait(barrier, 5)

    waits = []

    def send(sems, count, src_slot, dst_slot, half, k, target, own=False):
        first = pl.multiple_of(half * HALF + k * SUB, SUB)
        rows = pl.ds(first, SUB)
        src = tok.at[rows] if own else big.at[src_slot, rows]
        copy = pltpu.make_async_remote_copy(
            src_ref=src,
            dst_ref=big.at[dst_slot, rows],
            send_sem=sems.at[count],
            recv_sem=recv_sem.at[dst_slot, half * SUBS + k],
            device_id=target,
            device_id_type=MESH,
        )
        copy.start()
        waits.append(copy)

    def arrived(slot, half, k):
        first = pl.multiple_of(half * HALF + k * SUB, SUB)
        ref = big.at[slot, pl.ds(first, SUB)]
        pltpu.make_async_copy(ref, ref, recv_sem.at[slot, half * SUBS + k]).wait()

    ring_n = [0]
    side_n = [0]

    def ring(src_slot, half, k, target, own=False):
        send(ring_sem, ring_n[0], src_slot, src_slot, half, k, target, own)
        ring_n[0] += 1

    def side(src_slot, dst_slot, half, k, target, own=False):
        send(side_sem, side_n[0], src_slot, dst_slot, half, k, target, own)
        side_n[0] += 1

    def to_mate(slot, half, k, own=False):
        side(slot, slot + OTHER, half, k, mate, own)

    for k in range(SUBS):
        ring(y, 0, k, up, True)
        ring(y, 1, k, down, True)
    for k in range(SUBS):
        ring(y, 1, k, up, True)
        ring(y, 0, k, down, True)
    for half in range(2):
        for k in range(SUBS):
            to_mate(y, half, k, True)

    def pick(if_even, if_odd):
        return jnp.where(odd == 1, if_odd, if_even)

    def route(slot, half, k, cross, dst):
        side(
            slot,
            jnp.where(cross == 1, dst, slot + OTHER),
            half,
            k,
            tuple(jnp.where(cross == 1, a, b) for a, b in zip(side_to, mate)),
        )

    def step(s):
        plus, minus = slot_of(y - s), slot_of(y + s)
        for k in range(SUBS):
            arrived(plus, 0, k)
            if s < LONG:
                ring(plus, 0, k, up)
            arrived(minus, 1, k)
            if s < LONG:
                ring(minus, 1, k, down)
            if s == 1:
                route(plus, 0, k, 1 - odd, BND)
                route(minus, 1, k, odd, BND)
            elif s == 3:
                route(plus, 0, k, odd, BND + 1)
                route(minus, 1, k, 1 - odd, BND + 1)
            elif s == 4:
                to_mate(plus, 0, k)
                to_mate(minus, 1, k)
            elif s == 5:
                route(plus, 0, k, 1 - odd, BND + 1)
                route(minus, 1, k, odd, BND + 1)
        if s == 1:
            for k in range(SUBS):
                arrived(plus, 1, k)
                route(plus, 1, k, 1 - odd, BND)
                arrived(minus, 0, k)
                route(minus, 0, k, odd, BND)

    def bnd_arrived(which, half):
        for k in range(SUBS):
            arrived(BND + which, half, k)
            to_mate(BND + which, half, k)

    def mate_arrived(slot, half):
        for k in range(SUBS):
            arrived(slot + OTHER, half, k)

    g_near = half_id * 2
    g_far = (1 - half_id) * 2

    def project(near, far, half, run, with_query):
        rows = pl.ds(pl.multiple_of(half * HALF, HALF), HALF)
        parts = [(near, g_near + core), (near + OTHER, g_near + 1 - core), (far, g_far + core), (far + OTHER, g_far + 1 - core)]

        def tile(c):
            res = None
            for slot, g in parts:
                w = wbuf[pl.ds(pl.multiple_of(g * FEAT, FEAT), FEAT), c * 512:(c + 1) * 512]
                part = jnp.dot(big[slot, rows, :], w, preferred_element_type=jnp.float32)
                res = part if res is None else res + part
            return res.astype(jnp.bfloat16)

        if with_query:
            qbuf[rows, :] = tile(0)
        dst = pl.ds(pl.multiple_of(run * ROWS + half * HALF, HALF), HALF)
        kvbuf[dst, 0:512] = tile(1)
        kvbuf[dst, 512:1024] = tile(2)

    def make_bias():
        lane = lax.broadcasted_iota(jnp.int32, (BLOCK, BLOCK), 1)
        for p in range(4):
            cols = slice(p * BLOCK, (p + 1) * BLOCK)
            start = jnp.broadcast_to(bounds[0:1, cols].astype(jnp.float32), (BLOCK, BLOCK)).T.astype(jnp.int32)
            end = jnp.broadcast_to(bounds[1:2, cols].astype(jnp.float32), (BLOCK, BLOCK)).T.astype(jnp.int32)
            me = seq * 4 + p
            width, g0, g1 = win[me], glob[0, me], glob[1, me]
            for e in range(12):
                blk = seq * 4 - 4 + e
                ok = (abs(e - 4 - p) <= width) | (g0 == blk) | (g1 == blk)
                pos = jnp.where(ok, blk * BLOCK, -(1 << 20)) + lane
                keep = (pos >= start) & (pos < end)
                bias[cols, e * BLOCK:(e + 1) * BLOCK] = jnp.where(keep, 0.0, -jnp.inf)

    def attend(run, first_key, keys, is_first):
        k_rows = pl.ds(pl.multiple_of(run * ROWS + first_key, HALF), keys)

        def body(p, carry):
            q_rows = pl.ds(pl.multiple_of(p * BLOCK, BLOCK), BLOCK)
            mask = bias[q_rows, pl.ds(pl.multiple_of(run * ROWS + first_key, HALF), keys)]
            for h in range(HEADS):
                hc = slice(h * HEAD_DIM, (h + 1) * HEAD_DIM)
                key = kvbuf[k_rows, hc]
                value = kvbuf[k_rows, 512 + h * HEAD_DIM:512 + (h + 1) * HEAD_DIM]
                score = lax.dot_general(
                    qbuf[q_rows, hc], key, (((1,), (1,)), ((), ())), preferred_element_type=jnp.float32
                ) * HEAD_DIM ** -0.5 + mask
                high = jnp.broadcast_to(jnp.max(score, axis=1, keepdims=True), (BLOCK, HEAD_DIM))
                if not is_first:
                    old = top[h, q_rows, :]
                    high = jnp.maximum(high, old)
                expo = jnp.exp(score - high[:, 0:1])
                sums = jnp.broadcast_to(jnp.sum(expo, axis=1, keepdims=True), (BLOCK, HEAD_DIM))
                mixed = jnp.dot(expo.astype(jnp.bfloat16), value, preferred_element_type=jnp.float32)
                if not is_first:
                    keep = jnp.exp(old - high)
                    sums = sums + keep * total[h, q_rows, :]
                    mixed = mixed + keep * acc[h, q_rows, :]
                top[h, q_rows, :] = high
                total[h, q_rows, :] = sums
                acc[h, q_rows, :] = mixed
            return carry

        lax.fori_loop(0, 4, body, 0)

    even = 1 - odd
    h_f, h_b = odd, 1 - odd
    own_far = slot_of(y + 4)
    pair_near, pair_far = slot_of(y + sgn), slot_of(y - 3 * sgn)
    pair_run, bnd_run = 1 + sgn, 1 - sgn

    loads[1].wait()
    make_bias()
    step(1)
    for load in loads[2:] + loads[:1]:
        load.wait()
    step(2)
    bnd_arrived(0, h_f)
    bnd_arrived(0, h_b)
    step(3)
    for half in range(2):
        mate_arrived(y, half)
    mate_arrived(pair_near, h_f)
    mate_arrived(pair_far, h_f)
    project(pair_near, pair_far, h_f, pair_run, False)
    step(4)
    bnd_arrived(1, h_b)
    for half in range(2):
        mate_arrived(own_far, half)
        project(y, own_far, half, 1, True)
    attend(1, 0, ROWS, True)
    attend(pair_run, h_f * HALF, HALF, False)
    step(5)
    for half in (h_f, h_b):
        mate_arrived(BND, half)
    mate_arrived(BND + 1, h_b)
    project(BND + 1, BND, h_b, bnd_run, False)
    attend(bnd_run, h_b * HALF, HALF, False)
    mate_arrived(pair_near, h_b)
    mate_arrived(pair_far, h_b)
    project(pair_near, pair_far, h_b, pair_run, False)
    attend(pair_run, h_b * HALF, HALF, False)
    bnd_arrived(1, h_f)
    mate_arrived(BND + 1, h_f)
    project(BND + 1, BND, h_f, bnd_run, False)
    attend(bnd_run, h_f * HALF, HALF, False)
    for h in range(HEADS):
        out[:, h * HEAD_DIM:(h + 1) * HEAD_DIM] = (acc[h] / total[h]).astype(jnp.bfloat16)
    for copy in waits:
        copy.wait_send()


def local(groups, tokens, w_query, w_key, w_value, window, global_blocks, file_bounds):
    anywhere = pl.BlockSpec(memory_space=pl.ANY)
    scalars = pl.BlockSpec(memory_space=pltpu.SMEM)
    return pl.pallas_call(
        functools.partial(kernel, groups),
        out_shape=jax.ShapeDtypeStruct((ROWS, FEAT), jnp.bfloat16),
        in_specs=[anywhere] * 4 + [scalars] * 2 + [anywhere],
        out_specs=pl.BlockSpec(memory_space=pltpu.VMEM),
        scratch_shapes=[
            pltpu.VMEM((20, ROWS, FEAT), jnp.bfloat16),
            pltpu.VMEM((2048, 1536), jnp.bfloat16),
            pltpu.VMEM((ROWS, FEAT), jnp.bfloat16),
            pltpu.VMEM((3 * ROWS, 2 * FEAT), jnp.bfloat16),
            pltpu.VMEM((ROWS, 3 * ROWS), jnp.float32),
            pltpu.VMEM((2, ROWS), jnp.int32),
            pltpu.VMEM((HEADS, ROWS, HEAD_DIM), jnp.float32),
            pltpu.VMEM((HEADS, ROWS, HEAD_DIM), jnp.float32),
            pltpu.VMEM((HEADS, ROWS, HEAD_DIM), jnp.float32),
            pltpu.SemaphoreType.DMA((12 * SUBS,)),
            pltpu.SemaphoreType.DMA((16 * SUBS,)),
            pltpu.SemaphoreType.DMA((20, 2 * SUBS)),
            pltpu.SemaphoreType.DMA((5,)),
        ],
        compiler_params=pltpu.CompilerParams(
            collective_id=0, has_side_effects=True, vmem_limit_bytes=56 << 20
        ),
        cost_estimate=pl.CostEstimate(flops=9_000_000_000, bytes_accessed=8_000_000, transcendentals=3_000_000),
        name="gather_project_attend",
    )(tokens, w_query, w_key, w_value, window, global_blocks.T, file_bounds)


def solution(mesh):
    placed = (P("seq", "head"), P(None, "head"), P(None, "head"), P(None, "head"), P(), P(), P())
    return jax.shard_map(
        functools.partial(local, mesh.shape["seq"] // 4),
        mesh=mesh, in_specs=placed, out_specs=P("seq", "head"), check_vma=False,
    )
```

time: 175 us -> 85 us (0.49)
  the two profiles are of different devices: /device:TPU:25 before, /device:TPU:1 now
where the time goes in v1:
time: 85 us; the launch traced here: 84.8 us
  Pallas kernels  82.9 us (98%)
  local copies, waits for them, and re-layouts  1.87 us (2%)
    pallas_call x1, Pallas kernels, local(): pl.pallas_call(functools.partial(kernel, groups), out_shape=jax.ShapeDtyp...  82.9 us
    unnamed x1, local copies, waits for them, and re-layouts  1.87 us

profile of v1, /device:TPU:1, one launch (start us, length us, event | category | flops | bytes accessed | tf_op | source)
XLA Modules:
  0.0 84.8 jit_solution(8749805334534506141)
XLA Ops:
  0.0 82.9 %gather_project_attend.1 = bf16[512,512]{1,0:T(8,128)(2,1)} custom-call(bf16[512,512]{1,0:T(8,128)(2,1)} %tok.1, bf16[2048,512]{1,0:T(8,128)(2,1)} %wq.1, bf16[2048,512]{1,0:T(8,128)(2,1)} %wk.1, bf16[2048,512]{1,0:T(8,128)(2,1)} %wv.1, s32[768]{0:T(1024)} %win.1, s32[2,768]{1,0:T(2,128)} %bitcast.1, s32[2,98304]{1,0:T(2,128)} %fb.1), custom_call_target="tpu_custom_call" | custom-call | flops 8999999488 | bytes 8000000 | tf_op jit(solution)/shard_map/gather_project_attend/pallas_call | solution.py:277
  82.9 1.9 %copy.9 = bf16[512,512]{1,0:T(8,128)(2,1)} copy(bf16[512,512]{1,0:T(8,128)(2,1)} %gather_project_attend.1) | data formatting | bytes 1048576

commit v2 on v0

v2 whole, which is shorter than its diff:
```python
import functools

import jax
import jax.numpy as jnp
from jax import lax
from jax.experimental import pallas as pl
from jax.experimental.pallas import tpu as pltpu
from jax.sharding import PartitionSpec as P

MESH = pl.DeviceIdType.MESH
HEAD_DIM = 128
BLOCK = 128
ROWS = 512
FEAT = 512
HALF = 256
RING = 8
HEADS = 4
SUBS = 4
SUB = HALF // SUBS
BND = 8
OTHER = 10
LONG = 5
SCALE = HEAD_DIM ** -0.5 * 1.4426950408889634
LOW = -1e30


def kernel(groups, tok, wq, wk, wv, win, glob, fb, out, big, wbuf, qbuf, kbuf, vbuf, bias, bounds,
           part_own, part_pair, part_bnd, acc, top, ring_sem, side_sem, recv_sem, local_sem):
    seq = lax.axis_index("seq")
    head = lax.axis_index("head")
    group = seq // 4
    low = seq % 4
    half_id = head // 2
    core = head % 2
    y = half_id * 4 + low
    odd = low % 2
    sgn = 1 - 2 * odd
    h_f, h_b = odd, 1 - odd

    def slot_of(yy):
        return lax.rem(yy + 2 * RING, RING)

    def at(g, yy, c):
        yy = slot_of(yy)
        return (g * 4 + lax.rem(yy, 4), (yy // 4) * 2 + c)

    ahead, behind = at(group, y + sgn, core), at(group, y - sgn, core)
    mate = at(group, y, 1 - core)
    next_group = lax.rem(group + sgn + groups, groups)
    last_group = lax.rem(group - sgn + groups, groups)
    side, side_mate = at(next_group, y, core), at(next_group, y, 1 - core)

    own_first = pl.multiple_of(seq * ROWS, ROWS)
    load_tok = pltpu.make_async_copy(tok, big.at[y], local_sem.at[0])
    load_fb = pltpu.make_async_copy(fb.at[:, pl.ds(own_first, ROWS)], bounds, local_sem.at[1])
    load_w = [
        pltpu.make_async_copy(w, wbuf.at[:, pl.ds(i * FEAT, FEAT)], local_sem.at[2 + i])
        for i, w in enumerate((wq, wk, wv))
    ]

    barrier = pltpu.get_barrier_semaphore()
    peers = (ahead, behind, mate, side, side_mate, at(last_group, y, core), at(last_group, y, 1 - core))
    for peer in peers:
        pl.semaphore_signal(barrier, inc=1, device_id=peer, device_id_type=MESH)
    load_tok.start()
    load_fb.start()
    pl.semaphore_wait(barrier, len(peers))

    waits = []
    counts = {"ring": 0, "side": 0}

    def send(kind, src_slot, dst_slot, half, k, target, own=False):
        rows = pl.ds(pl.multiple_of(half * HALF + k * SUB, SUB), SUB)
        copy = pltpu.make_async_remote_copy(
            src_ref=tok.at[rows] if own else big.at[src_slot, rows],
            dst_ref=big.at[dst_slot, rows],
            send_sem=(ring_sem if kind == "ring" else side_sem).at[counts[kind]],
            recv_sem=recv_sem.at[dst_slot, half * SUBS + k],
            device_id=target,
            device_id_type=MESH,
        )
        copy.start()
        counts[kind] += 1
        waits.append(copy)

    def to_mate(slot, half, k, own=False):
        send("side", slot, slot + OTHER, half, k, mate, own)

    def arrived(slot, half, k):
        ref = big.at[slot, pl.ds(pl.multiple_of(half * HALF + k * SUB, SUB), SUB)]
        pltpu.make_async_copy(ref, ref, recv_sem.at[slot, half * SUBS + k]).wait()

    def mate_arrived(slot, half):
        for k in range(SUBS):
            arrived(slot + OTHER, half, k)

    def bnd_arrived(which, half):
        for k in range(SUBS):
            arrived(BND + which, half, k)
            to_mate(BND + which, half, k)

    def step(s, pieces=range(SUBS)):
        f, b = slot_of(y - s * sgn), slot_of(y + s * sgn)
        for k in pieces:
            arrived(f, h_f, k)
            if s < LONG:
                send("ring", f, f, h_f, k, ahead)
            if s == 1:
                send("side", f, BND, h_f, k, side)
            elif s in (3, 4):
                to_mate(f, h_f, k)
            elif s == 5:
                send("side", f, BND + 1, h_f, k, side)
                send("side", f, BND + 1 + OTHER, h_f, k, side_mate)
            arrived(b, h_b, k)
            if s < LONG:
                send("ring", b, b, h_b, k, behind)
            if s == 3:
                send("side", b, BND + 1, h_b, k, side)
            elif s != 2:
                to_mate(b, h_b, k)
        if s == 1:
            for k in pieces:
                arrived(f, h_b, k)
                send("side", f, BND, h_b, k, side)
                arrived(b, h_f, k)
                to_mate(b, h_f, k)

    g_near = half_id * 2
    g_far = 2 - g_near

    def rows_of(half):
        return pl.ds(pl.multiple_of(half * HALF, HALF), HALF)

    def product(slot, g, half, tile):
        def one(s, gg):
            w = wbuf[pl.ds(pl.multiple_of(gg * FEAT, FEAT), FEAT), tile * FEAT:(tile + 1) * FEAT]
            return jnp.dot(big[s, rows_of(half), :], w, preferred_element_type=jnp.float32)

        return one(slot, g + core) + one(slot + OTHER, g + 1 - core)

    def first_part(part, slot, g, half, tiles):
        for i, tile in enumerate(tiles):
            part[rows_of(half), i * FEAT:(i + 1) * FEAT] = product(slot, g, half, tile)

    def second_part(part, slot, g, half, tiles, run):
        keys = pl.ds(pl.multiple_of(run * ROWS + half * HALF, HALF), HALF)
        for i, tile in enumerate(tiles):
            whole = part[rows_of(half), i * FEAT:(i + 1) * FEAT] + product(slot, g, half, tile)
            if tile == 0:
                qbuf[rows_of(half), :] = whole.astype(jnp.bfloat16)
            elif tile == 1:
                kbuf[keys, :] = whole.astype(jnp.bfloat16)
            else:
                for h in range(HEADS):
                    vbuf[h, 0:HEAD_DIM, keys] = whole[:, h * HEAD_DIM:(h + 1) * HEAD_DIM].T.astype(jnp.bfloat16)

    def make_bias():
        for e in range(12):
            blk = seq * 4 - 4 + e
            row = lax.broadcasted_iota(jnp.int32, (BLOCK, BLOCK), 0)
            for p in range(4):
                cols = slice(p * BLOCK, (p + 1) * BLOCK)
                me = seq * 4 + p
                ok = (abs(e - 4 - p) <= win[me]) | (glob[0, me] == blk) | (glob[1, me] == blk)
                pos = jnp.where(ok, blk * BLOCK, -(1 << 20)) + row
                keep = (pos >= bounds[0:1, cols]) & (pos < bounds[1:2, cols])
                bias[e * BLOCK:(e + 1) * BLOCK, cols] = jnp.where(keep, 0.0, -jnp.inf)

    def attend(run, first_key, keys, query_half=None, heads=range(HEADS)):
        k_rows = pl.ds(pl.multiple_of(run * ROWS + first_key, HALF), keys)
        q_rows = slice(None) if query_half is None else rows_of(query_half)
        mask = bias[k_rows, q_rows]
        for h in heads:
            hc = slice(h * HEAD_DIM, (h + 1) * HEAD_DIM)
            score = lax.dot_general(
                kbuf[k_rows, hc], qbuf[q_rows, hc], (((1,), (1,)), ((), ())), preferred_element_type=jnp.float32
            ) + mask
            old = top[h, :, q_rows]
            high = jnp.maximum(jnp.max(score, axis=0, keepdims=True), old)
            expo = jnp.exp2((score - high) * SCALE).astype(jnp.bfloat16)
            mixed = jnp.dot(vbuf[h, :, k_rows], expo, preferred_element_type=jnp.float32)
            acc[h, :, q_rows] = mixed + jnp.exp2((old - high) * SCALE) * acc[h, :, q_rows]
            top[h, :, q_rows] = high

    def finish(half):
        for h in range(HEADS):
            mean = acc[h, 0:HEAD_DIM, rows_of(half)] / acc[h, HEAD_DIM:HEAD_DIM + 1, rows_of(half)]
            out[rows_of(half), h * HEAD_DIM:(h + 1) * HEAD_DIM] = mean.T.astype(jnp.bfloat16)

    own_far = slot_of(y + 4)
    pair_near, pair_far = slot_of(y + sgn), slot_of(y - 3 * sgn)
    pair_run, bnd_run = 1 + sgn, 1 - sgn
    both, keyval = (0, 1), (1, 2)

    for k in range(SUBS):
        send("ring", y, y, h_f, k, ahead, True)
        send("ring", y, y, h_b, k, behind, True)
    for k in range(SUBS):
        send("ring", y, y, h_b, k, ahead, True)
        send("ring", y, y, h_f, k, behind, True)
    for half in both:
        for k in range(SUBS):
            to_mate(y, half, k, True)
    for load in load_w:
        load.start()
    acc[...] = jnp.zeros_like(acc)
    top[...] = jnp.full_like(top, LOW)
    vbuf[:, HEAD_DIM:, :] = jnp.ones_like(vbuf[:, HEAD_DIM:, :])
    load_fb.wait()
    make_bias()
    for load in load_w:
        load.wait()
    load_tok.wait()
    for half in both:
        mate_arrived(y, half)
        first_part(part_own, y, g_near, half, (0, 1, 2))
    step(1)
    for half in both:
        mate_arrived(pair_near, half)
        first_part(part_pair, pair_near, g_near, half, keyval)
    step(2)
    for half in (h_f, h_b):
        bnd_arrived(0, half)
    step(3)
    for half in (h_f, h_b):
        mate_arrived(BND, half)
        first_part(part_bnd, BND, g_far, half, keyval)
    mate_arrived(pair_far, h_f)
    second_part(part_pair, pair_far, g_far, h_f, keyval, pair_run)
    step(4)
    bnd_arrived(1, h_b)
    for half in both:
        mate_arrived(own_far, half)
        second_part(part_own, own_far, g_far, half, (0, 1, 2), 1)
    step(5, (0,))
    attend(1, 0, ROWS, None, (0, 1))
    step(5, (1,))
    attend(1, 0, ROWS, None, (2, 3))
    step(5, (2,))
    mate_arrived(BND + 1, h_b)
    second_part(part_bnd, BND + 1, g_near, h_b, keyval, bnd_run)
    step(5, (3,))
    attend(pair_run, h_f * HALF, HALF)
    attend(bnd_run, h_b * HALF, HALF)
    mate_arrived(pair_far, h_b)
    second_part(part_pair, pair_far, g_far, h_b, keyval, pair_run)
    attend(pair_run, h_b * HALF, HALF, h_b)
    finish(h_b)
    for k in range(SUBS):
        arrived(BND + 1, h_f, k)
    mate_arrived(BND + 1, h_f)
    second_part(part_bnd, BND + 1, g_near, h_f, keyval, bnd_run)
    attend(bnd_run, h_f * HALF, HALF, h_f)
    finish(h_f)
    for copy in waits:
        copy.wait_send()


def local(groups, tokens, w_query, w_key, w_value, window, global_blocks, file_bounds):
    anywhere = pl.BlockSpec(memory_space=pl.ANY)
    scalars = pl.BlockSpec(memory_space=pltpu.SMEM)
    return pl.pallas_call(
        functools.partial(kernel, groups),
        out_shape=jax.ShapeDtypeStruct((ROWS, FEAT), jnp.bfloat16),
        in_specs=[anywhere] * 4 + [scalars] * 2 + [anywhere],
        out_specs=pl.BlockSpec(memory_space=pltpu.VMEM),
        scratch_shapes=[
            pltpu.VMEM((20, ROWS, FEAT), jnp.bfloat16),
            pltpu.VMEM((2048, 3 * FEAT), jnp.bfloat16),
            pltpu.VMEM((ROWS, FEAT), jnp.bfloat16),
            pltpu.VMEM((3 * ROWS, FEAT), jnp.bfloat16),
            pltpu.VMEM((HEADS, HEAD_DIM + 16, 3 * ROWS), jnp.bfloat16),
            pltpu.VMEM((3 * ROWS, ROWS), jnp.float32),
            pltpu.VMEM((2, ROWS), jnp.int32),
            pltpu.VMEM((ROWS, 3 * FEAT), jnp.float32),
            pltpu.VMEM((ROWS, 2 * FEAT), jnp.float32),
            pltpu.VMEM((ROWS, 2 * FEAT), jnp.float32),
            pltpu.VMEM((HEADS, HEAD_DIM + 16, ROWS), jnp.float32),
            pltpu.VMEM((HEADS, 1, ROWS), jnp.float32),
            pltpu.SemaphoreType.DMA((12 * SUBS,)),
            pltpu.SemaphoreType.DMA((16 * SUBS,)),
            pltpu.SemaphoreType.DMA((20, 2 * SUBS)),
            pltpu.SemaphoreType.DMA((5,)),
        ],
        compiler_params=pltpu.CompilerParams(
            collective_id=0, has_side_effects=True, vmem_limit_bytes=56 << 20
        ),
        cost_estimate=pl.CostEstimate(flops=9_000_000_000, bytes_accessed=8_000_000, transcendentals=3_000_000),
        name="gather_project_attend",
    )(tokens, w_query, w_key, w_value, window, global_blocks.T, file_bounds)


def solution(mesh):
    placed = (P("seq", "head"), P(None, "head"), P(None, "head"), P(None, "head"), P(), P(), P())
    return jax.shard_map(
        functools.partial(local, mesh.shape["seq"] // 4),
        mesh=mesh, in_specs=placed, out_specs=P("seq", "head"), check_vma=False,
    )
```

time: 175 us -> 74.5 us (0.43)
  the two profiles are of different devices: /device:TPU:25 before, /device:TPU:1 now
where the time goes in v2:
time: 74.5 us; the launch traced here: 74.2 us
  Pallas kernels  72.4 us (97%)
  local copies, waits for them, and re-layouts  1.87 us (3%)
    pallas_call x1, Pallas kernels, local(): pl.pallas_call(functools.partial(kernel, groups), out_shape=jax.ShapeDtyp...  72.4 us
    unnamed x1, local copies, waits for them, and re-layouts  1.87 us

profile of v2, /device:TPU:1, one launch (start us, length us, event | category | flops | bytes accessed | tf_op | source)
XLA Modules:
  0.0 74.2 jit_solution(4503789577665143337)
XLA Ops:
  0.0 72.4 %gather_project_attend.1 = bf16[512,512]{1,0:T(8,128)(2,1)} custom-call(bf16[512,512]{1,0:T(8,128)(2,1)} %tok.1, bf16[2048,512]{1,0:T(8,128)(2,1)} %wq.1, bf16[2048,512]{1,0:T(8,128)(2,1)} %wk.1, bf16[2048,512]{1,0:T(8,128)(2,1)} %wv.1, s32[768]{0:T(1024)} %win.1, s32[2,768]{1,0:T(2,128)} %bitcast.1, s32[2,98304]{1,0:T(2,128)} %fb.1), custom_call_target="tpu_custom_call" | custom-call | flops 8999999488 | bytes 8000000 | tf_op jit(solution)/shard_map/gather_project_attend/pallas_call | solution.py:263
  72.4 1.9 %copy.9 = bf16[512,512]{1,0:T(8,128)(2,1)} copy(bf16[512,512]{1,0:T(8,128)(2,1)} %gather_project_attend.1) | data formatting | bytes 1048576

commit v3 on v2

--- a/solution.py
+++ b/solution.py
@@ -48,7 +48,7 @@
     mate = at(group, y, 1 - core)
     next_group = lax.rem(group + sgn + groups, groups)
     last_group = lax.rem(group - sgn + groups, groups)
-    side, side_mate = at(next_group, y, core), at(next_group, y, 1 - core)
+    side = at(next_group, y, core)
 
     own_first = pl.multiple_of(seq * ROWS, ROWS)
     load_tok = pltpu.make_async_copy(tok, big.at[y], local_sem.at[0])
@@ -59,7 +59,7 @@
     ]
 
     barrier = pltpu.get_barrier_semaphore()
-    peers = (ahead, behind, mate, side, side_mate, at(last_group, y, core), at(last_group, y, 1 - core))
+    peers = (ahead, behind, mate, side, at(last_group, y, core))
     for peer in peers:
         pl.semaphore_signal(barrier, inc=1, device_id=peer, device_id_type=MESH)
     load_tok.start()
@@ -69,13 +69,18 @@
     waits = []
     counts = {"ring": 0, "side": 0}
 
+    def rows_of(half, k=None):
+        if k is None:
+            return pl.ds(pl.multiple_of(half * HALF, HALF), HALF)
+        return pl.ds(pl.multiple_of(half * HALF + k * SUB, SUB), SUB)
+
     def send(kind, src_slot, dst_slot, half, k, target, own=False):
-        rows = pl.ds(pl.multiple_of(half * HALF + k * SUB, SUB), SUB)
+        rows = rows_of(half, k)
         copy = pltpu.make_async_remote_copy(
             src_ref=tok.at[rows] if own else big.at[src_slot, rows],
             dst_ref=big.at[dst_slot, rows],
             send_sem=(ring_sem if kind == "ring" else side_sem).at[counts[kind]],
-            recv_sem=recv_sem.at[dst_slot, half * SUBS + k],
+            recv_sem=recv_sem.at[dst_slot, half * SUBS + (k or 0)],
             device_id=target,
             device_id_type=MESH,
         )
@@ -83,21 +88,15 @@
         counts[kind] += 1
         waits.append(copy)
 
-    def to_mate(slot, half, k, own=False):
+    def to_mate(slot, half, own=False, k=None):
         send("side", slot, slot + OTHER, half, k, mate, own)
 
-    def arrived(slot, half, k):
-        ref = big.at[slot, pl.ds(pl.multiple_of(half * HALF + k * SUB, SUB), SUB)]
-        pltpu.make_async_copy(ref, ref, recv_sem.at[slot, half * SUBS + k]).wait()
+    def arrived(slot, half, k=None):
+        ref = big.at[slot, rows_of(half, k)]
+        pltpu.make_async_copy(ref, ref, recv_sem.at[slot, half * SUBS + (k or 0)]).wait()
 
     def mate_arrived(slot, half):
-        for k in range(SUBS):
-            arrived(slot + OTHER, half, k)
-
-    def bnd_arrived(which, half):
-        for k in range(SUBS):
-            arrived(BND + which, half, k)
-            to_mate(BND + which, half, k)
+        arrived(slot + OTHER, half)
 
     def step(s, pieces=range(SUBS)):
         f, b = slot_of(y - s * sgn), slot_of(y + s * sgn)
@@ -105,32 +104,34 @@
             arrived(f, h_f, k)
             if s < LONG:
                 send("ring", f, f, h_f, k, ahead)
-            if s == 1:
-                send("side", f, BND, h_f, k, side)
-            elif s in (3, 4):
-                to_mate(f, h_f, k)
-            elif s == 5:
+            else:
                 send("side", f, BND + 1, h_f, k, side)
-                send("side", f, BND + 1 + OTHER, h_f, k, side_mate)
             arrived(b, h_b, k)
             if s < LONG:
                 send("ring", b, b, h_b, k, behind)
-            if s == 3:
-                send("side", b, BND + 1, h_b, k, side)
-            elif s != 2:
-                to_mate(b, h_b, k)
+        if SUBS - 1 not in pieces:
+            return
         if s == 1:
-            for k in pieces:
-                arrived(f, h_b, k)
-                send("side", f, BND, h_b, k, side)
-                arrived(b, h_f, k)
-                to_mate(b, h_f, k)
+            send("side", f, BND, h_f, None, side)
+        elif s in (3, 4):
+            to_mate(f, h_f)
+        if s == 3:
+            send("side", b, BND + 1, h_b, None, side)
+        elif s != 2:
+            to_mate(b, h_b)
+    def short_way():
+        f, b = slot_of(y - sgn), slot_of(y + sgn)
+        arrived(f, h_b)
+        send("side", f, BND, h_b, None, side)
+        arrived(b, h_f)
+        to_mate(b, h_f)
+
+    def bnd_arrived(k):
+        arrived(BND + 1, h_f, k)
+        to_mate(BND + 1, h_f, False, k)
 
     g_near = half_id * 2
     g_far = 2 - g_near
-
-    def rows_of(half):
-        return pl.ds(pl.multiple_of(half * HALF, HALF), HALF)
 
     def product(slot, g, half, tile):
         def one(s, gg):
@@ -196,12 +197,8 @@
     for k in range(SUBS):
         send("ring", y, y, h_f, k, ahead, True)
         send("ring", y, y, h_b, k, behind, True)
-    for k in range(SUBS):
-        send("ring", y, y, h_b, k, ahead, True)
-        send("ring", y, y, h_f, k, behind, True)
     for half in both:
-        for k in range(SUBS):
-            to_mate(y, half, k, True)
+        to_mate(y, half, True)
     for load in load_w:
         load.start()
     acc[...] = jnp.zeros_like(acc)
@@ -209,47 +206,59 @@
     vbuf[:, HEAD_DIM:, :] = jnp.ones_like(vbuf[:, HEAD_DIM:, :])
     load_fb.wait()
     make_bias()
+    load_tok.wait()
+    step(1)
     for load in load_w:
         load.wait()
-    load_tok.wait()
-    for half in both:
-        mate_arrived(y, half)
-        first_part(part_own, y, g_near, half, (0, 1, 2))
-    step(1)
-    for half in both:
-        mate_arrived(pair_near, half)
-        first_part(part_pair, pair_near, g_near, half, keyval)
+    mate_arrived(y, 0)
+    first_part(part_own, y, g_near, 0, (0, 1, 2))
     step(2)
-    for half in (h_f, h_b):
-        bnd_arrived(0, half)
+    arrived(BND, h_f)
+    to_mate(BND, h_f)
+    mate_arrived(y, 1)
+    first_part(part_own, y, g_near, 1, (0, 1, 2))
+    mate_arrived(pair_near, h_b)
+    first_part(part_pair, pair_near, g_near, h_b, keyval)
     step(3)
-    for half in (h_f, h_b):
-        mate_arrived(BND, half)
-        first_part(part_bnd, BND, g_far, half, keyval)
+    send("ring", y, y, h_b, None, ahead, True)
+    send("ring", y, y, h_f, None, behind, True)
+    mate_arrived(BND, h_f)
+    first_part(part_bnd, BND, g_far, h_f, keyval)
     mate_arrived(pair_far, h_f)
-    second_part(part_pair, pair_far, g_far, h_f, keyval, pair_run)
+    first_part(part_pair, pair_far, g_far, h_f, keyval)
     step(4)
-    bnd_arrived(1, h_b)
+    arrived(BND + 1, h_b)
+    to_mate(BND + 1, h_b)
     for half in both:
         mate_arrived(own_far, half)
         second_part(part_own, own_far, g_far, half, (0, 1, 2), 1)
+    attend(1, 0, ROWS, None, (0, 1))
+    short_way()
+    attend(1, 0, ROWS, None, (2, 3))
     step(5, (0,))
-    attend(1, 0, ROWS, None, (0, 1))
+    mate_arrived(BND + 1, h_b)
+    first_part(part_bnd, BND + 1, g_near, h_b, keyval)
     step(5, (1,))
-    attend(1, 0, ROWS, None, (2, 3))
+    mate_arrived(pair_near, h_f)
+    second_part(part_pair, pair_near, g_near, h_f, keyval, pair_run)
     step(5, (2,))
-    mate_arrived(BND + 1, h_b)
-    second_part(part_bnd, BND + 1, g_near, h_b, keyval, bnd_run)
+    arrived(BND, h_b)
+    to_mate(BND, h_b)
+    attend(pair_run, h_f * HALF, HALF)
     step(5, (3,))
-    attend(pair_run, h_f * HALF, HALF)
+    mate_arrived(BND, h_b)
+    second_part(part_bnd, BND, g_far, h_b, keyval, bnd_run)
+    bnd_arrived(0)
+    bnd_arrived(1)
     attend(bnd_run, h_b * HALF, HALF)
+    bnd_arrived(2)
     mate_arrived(pair_far, h_b)
     second_part(part_pair, pair_far, g_far, h_b, keyval, pair_run)
+    bnd_arrived(3)
     attend(pair_run, h_b * HALF, HALF, h_b)
     finish(h_b)
     for k in range(SUBS):
-        arrived(BND + 1, h_f, k)
-    mate_arrived(BND + 1, h_f)
+        arrived(BND + 1 + OTHER, h_f, k)
     second_part(part_bnd, BND + 1, g_near, h_f, keyval, bnd_run)
     attend(bnd_run, h_f * HALF, HALF, h_f)
     finish(h_f)
@@ -262,7 +271,7 @@
     scalars = pl.BlockSpec(memory_space=pltpu.SMEM)
     return pl.pallas_call(
         functools.partial(kernel, groups),
-        out_shape=jax.ShapeDtypeStruct((ROWS, FEAT), jnp.bfloat16),
+        out_shape=pltpu.VMEM((ROWS, FEAT), jnp.bfloat16),
         in_specs=[anywhere] * 4 + [scalars] * 2 + [anywhere],
         out_specs=pl.BlockSpec(memory_space=pltpu.VMEM),
         scratch_shapes=[
@@ -278,8 +287,8 @@
             pltpu.VMEM((ROWS, 2 * FEAT), jnp.float32),
             pltpu.VMEM((HEADS, HEAD_DIM + 16, ROWS), jnp.float32),
             pltpu.VMEM((HEADS, 1, ROWS), jnp.float32),
-            pltpu.SemaphoreType.DMA((12 * SUBS,)),
-            pltpu.SemaphoreType.DMA((16 * SUBS,)),
+            pltpu.SemaphoreType.DMA((10 * SUBS + 2,)),
+            pltpu.SemaphoreType.DMA((14 + 2 * SUBS,)),
             pltpu.SemaphoreType.DMA((20, 2 * SUBS)),
             pltpu.SemaphoreType.DMA((5,)),
         ],

time: 74.5 us -> 72.3 us (0.970)
  Pallas kernels: 72.4 us -> 71.3 us
  local copies, waits for them, and re-layouts: 1.87 us -> 0.8 us
    unnamed x1, local copies, waits for them, and re-layouts: 1.87 us -> 0.8 us
    pallas_call x1, Pallas kernels: 72.4 us -> 71.3 us  [local(): pl.pallas_call(functools.partial(kernel, groups), out_shape=pltpu.VMEM((R...]
where the time goes in v3:
time: 72.3 us; the launch traced here: 72.1 us
  Pallas kernels  71.3 us (99%)
  local copies, waits for them, and re-layouts  0.8 us (1%)
    pallas_call x1, Pallas kernels, local(): pl.pallas_call(functools.partial(kernel, groups), out_shape=pltpu.VMEM((R...  71.3 us

profile of v3, /device:TPU:1, one launch (start us, length us, event | category | flops | bytes accessed | tf_op | source)
XLA Modules:
  0.0 72.1 jit_solution(6666593350326068562)
XLA Ops:
  0.0 71.3 %gather_project_attend.1 = bf16[512,512]{1,0:T(8,128)(2,1)S(1)} custom-call(bf16[512,512]{1,0:T(8,128)(2,1)} %tok.1, bf16[2048,512]{1,0:T(8,128)(2,1)} %wq.1, bf16[2048,512]{1,0:T(8,128)(2,1)} %wk.1, bf16[2048,512]{1,0:T(8,128)(2,1)} %wv.1, s32[768]{0:T(1024)} %win.1, s32[2,768]{1,0:T(2,128)} %bitcast.1, s32[2,98304]{1,0:T(2,128)} %fb.1), custom_call_target="tpu_custom_call" | custom-call | flops 8999999488 | bytes 8000000 | tf_op jit(solution)/shard_map/gather_project_attend/pallas_call | solution.py:272
  71.3 0.8 %copy.9 = bf16[512,512]{1,0:T(8,128)(2,1)} copy(bf16[512,512]{1,0:T(8,128)(2,1)S(1)} %gather_project_attend.1) | data formatting | bytes 1048576

commit v4 on v3

--- a/solution.py
+++ b/solution.py
@@ -51,7 +51,9 @@
     side = at(next_group, y, core)
 
     own_first = pl.multiple_of(seq * ROWS, ROWS)
-    load_tok = pltpu.make_async_copy(tok, big.at[y], local_sem.at[0])
+    mine = pl.ds(pl.multiple_of(core * FEAT, FEAT), FEAT)
+    theirs = pl.ds(pl.multiple_of((1 - core) * FEAT, FEAT), FEAT)
+    load_tok = pltpu.make_async_copy(tok, big.at[y, :, mine], local_sem.at[0])
     load_fb = pltpu.make_async_copy(fb.at[:, pl.ds(own_first, ROWS)], bounds, local_sem.at[1])
     load_w = [
         pltpu.make_async_copy(w, wbuf.at[:, pl.ds(i * FEAT, FEAT)], local_sem.at[2 + i])
@@ -76,11 +78,12 @@
 
     def send(kind, src_slot, dst_slot, half, k, target, own=False):
         rows = rows_of(half, k)
+        to = dst_slot + (OTHER if target is mate else 0)
         copy = pltpu.make_async_remote_copy(
-            src_ref=tok.at[rows] if own else big.at[src_slot, rows],
-            dst_ref=big.at[dst_slot, rows],
+            src_ref=tok.at[rows] if own else big.at[src_slot, rows, mine],
+            dst_ref=big.at[dst_slot, rows, mine],
             send_sem=(ring_sem if kind == "ring" else side_sem).at[counts[kind]],
-            recv_sem=recv_sem.at[dst_slot, half * SUBS + (k or 0)],
+            recv_sem=recv_sem.at[to, half * SUBS + (k or 0)],
             device_id=target,
             device_id_type=MESH,
         )
@@ -88,15 +91,16 @@
         counts[kind] += 1
         waits.append(copy)
 
-    def to_mate(slot, half, own=False, k=None):
-        send("side", slot, slot + OTHER, half, k, mate, own)
+    def to_mate(slot, half, k=None, own=False):
+        send("side", slot, slot, half, k, mate, own)
 
     def arrived(slot, half, k=None):
-        ref = big.at[slot, rows_of(half, k)]
+        ref = big.at[slot, rows_of(half, k), mine]
         pltpu.make_async_copy(ref, ref, recv_sem.at[slot, half * SUBS + (k or 0)]).wait()
 
-    def mate_arrived(slot, half):
-        arrived(slot + OTHER, half)
+    def mate_arrived(slot, half, k=None):
+        ref = big.at[slot, rows_of(half, k), theirs]
+        pltpu.make_async_copy(ref, ref, recv_sem.at[slot + OTHER, half * SUBS + (k or 0)]).wait()
 
     def step(s, pieces=range(SUBS)):
         f, b = slot_of(y - s * sgn), slot_of(y + s * sgn)
@@ -119,26 +123,25 @@
             send("side", b, BND + 1, h_b, None, side)
         elif s != 2:
             to_mate(b, h_b)
-    def short_way():
+
+    def short_way(k):
         f, b = slot_of(y - sgn), slot_of(y + sgn)
-        arrived(f, h_b)
-        send("side", f, BND, h_b, None, side)
-        arrived(b, h_f)
-        to_mate(b, h_f)
-
-    def bnd_arrived(k):
-        arrived(BND + 1, h_f, k)
-        to_mate(BND + 1, h_f, False, k)
+        arrived(f, h_b, k)
+        send("side", f, BND, h_b, k, side)
+        arrived(b, h_f, k)
+        if k == SUBS - 1:
+            to_mate(b, h_f)
+
+    def bnd_arrived(which, half, k=None):
+        arrived(BND + which, half, k)
+        to_mate(BND + which, half, k)
 
     g_near = half_id * 2
     g_far = 2 - g_near
 
     def product(slot, g, half, tile):
-        def one(s, gg):
-            w = wbuf[pl.ds(pl.multiple_of(gg * FEAT, FEAT), FEAT), tile * FEAT:(tile + 1) * FEAT]
-            return jnp.dot(big[s, rows_of(half), :], w, preferred_element_type=jnp.float32)
-
-        return one(slot, g + core) + one(slot + OTHER, g + 1 - core)
+        w = wbuf[pl.ds(pl.multiple_of(g * FEAT, 2 * FEAT), 2 * FEAT), tile * FEAT:(tile + 1) * FEAT]
+        return jnp.dot(big[slot, rows_of(half), :], w, preferred_element_type=jnp.float32)
 
     def first_part(part, slot, g, half, tiles):
         for i, tile in enumerate(tiles):
@@ -198,7 +201,7 @@
         send("ring", y, y, h_f, k, ahead, True)
         send("ring", y, y, h_b, k, behind, True)
     for half in both:
-        to_mate(y, half, True)
+        to_mate(y, half, None, True)
     for load in load_w:
         load.start()
     acc[...] = jnp.zeros_like(acc)
@@ -213,52 +216,56 @@
     mate_arrived(y, 0)
     first_part(part_own, y, g_near, 0, (0, 1, 2))
     step(2)
-    arrived(BND, h_f)
-    to_mate(BND, h_f)
     mate_arrived(y, 1)
     first_part(part_own, y, g_near, 1, (0, 1, 2))
+    step(3)
+    for k in range(SUBS):
+        send("ring", y, y, h_b, k, ahead, True)
+        send("ring", y, y, h_f, k, behind, True)
+    bnd_arrived(0, h_f)
     mate_arrived(pair_near, h_b)
     first_part(part_pair, pair_near, g_near, h_b, keyval)
-    step(3)
-    send("ring", y, y, h_b, None, ahead, True)
-    send("ring", y, y, h_f, None, behind, True)
     mate_arrived(BND, h_f)
     first_part(part_bnd, BND, g_far, h_f, keyval)
     mate_arrived(pair_far, h_f)
     first_part(part_pair, pair_far, g_far, h_f, keyval)
     step(4)
-    arrived(BND + 1, h_b)
-    to_mate(BND + 1, h_b)
-    for half in both:
-        mate_arrived(own_far, half)
-        second_part(part_own, own_far, g_far, half, (0, 1, 2), 1)
+    short_way(0)
+    mate_arrived(own_far, 0)
+    second_part(part_own, own_far, g_far, 0, (0, 1, 2), 1)
+    short_way(1)
+    bnd_arrived(1, h_b)
+    mate_arrived(own_far, 1)
+    second_part(part_own, own_far, g_far, 1, (0, 1, 2), 1)
+    short_way(2)
     attend(1, 0, ROWS, None, (0, 1))
-    short_way()
+    short_way(3)
     attend(1, 0, ROWS, None, (2, 3))
     step(5, (0,))
     mate_arrived(BND + 1, h_b)
     first_part(part_bnd, BND + 1, g_near, h_b, keyval)
     step(5, (1,))
+    for k in range(SUBS):
+        arrived(BND, h_b, k)
+    to_mate(BND, h_b)
     mate_arrived(pair_near, h_f)
     second_part(part_pair, pair_near, g_near, h_f, keyval, pair_run)
     step(5, (2,))
-    arrived(BND, h_b)
-    to_mate(BND, h_b)
     attend(pair_run, h_f * HALF, HALF)
     step(5, (3,))
+    bnd_arrived(1, h_f, 0)
     mate_arrived(BND, h_b)
     second_part(part_bnd, BND, g_far, h_b, keyval, bnd_run)
-    bnd_arrived(0)
-    bnd_arrived(1)
+    bnd_arrived(1, h_f, 1)
     attend(bnd_run, h_b * HALF, HALF)
-    bnd_arrived(2)
+    bnd_arrived(1, h_f, 2)
     mate_arrived(pair_far, h_b)
     second_part(part_pair, pair_far, g_far, h_b, keyval, pair_run)
-    bnd_arrived(3)
+    bnd_arrived(1, h_f, 3)
     attend(pair_run, h_b * HALF, HALF, h_b)
     finish(h_b)
     for k in range(SUBS):
-        arrived(BND + 1 + OTHER, h_f, k)
+        mate_arrived(BND + 1, h_f, k)
     second_part(part_bnd, BND + 1, g_near, h_f, keyval, bnd_run)
     attend(bnd_run, h_f * HALF, HALF, h_f)
     finish(h_f)
@@ -275,7 +282,7 @@
         in_specs=[anywhere] * 4 + [scalars] * 2 + [anywhere],
         out_specs=pl.BlockSpec(memory_space=pltpu.VMEM),
         scratch_shapes=[
-            pltpu.VMEM((20, ROWS, FEAT), jnp.bfloat16),
+            pltpu.VMEM((10, ROWS, 2 * FEAT), jnp.bfloat16),
             pltpu.VMEM((2048, 3 * FEAT), jnp.bfloat16),
             pltpu.VMEM((ROWS, FEAT), jnp.bfloat16),
             pltpu.VMEM((3 * ROWS, FEAT), jnp.bfloat16),
@@ -287,8 +294,8 @@
             pltpu.VMEM((ROWS, 2 * FEAT), jnp.float32),
             pltpu.VMEM((HEADS, HEAD_DIM + 16, ROWS), jnp.float32),
             pltpu.VMEM((HEADS, 1, ROWS), jnp.float32),
-            pltpu.SemaphoreType.DMA((10 * SUBS + 2,)),
-            pltpu.SemaphoreType.DMA((14 + 2 * SUBS,)),
+            pltpu.SemaphoreType.DMA((12 * SUBS,)),
+            pltpu.SemaphoreType.DMA((13 + 3 * SUBS,)),
             pltpu.SemaphoreType.DMA((20, 2 * SUBS)),
             pltpu.SemaphoreType.DMA((5,)),
         ],

time: 72.3 us -> 67.1 us (0.928)
  Pallas kernels: 71.3 us -> 66.1 us
    pallas_call x1, Pallas kernels: 71.3 us -> 66.1 us  [local(): pl.pallas_call(functools.partial(kernel, groups), out_shape=pltpu.VMEM((R...]
where the time goes in v4:
time: 67.1 us; the launch traced here: 66.9 us
  Pallas kernels  66.1 us (99%)
  local copies, waits for them, and re-layouts  0.8 us (1%)
    pallas_call x1, Pallas kernels, local(): pl.pallas_call(functools.partial(kernel, groups), out_shape=pltpu.VMEM((R...  66.1 us

profile of v4, /device:TPU:1, one launch (start us, length us, event | category | flops | bytes accessed | tf_op | source)
XLA Modules:
  0.0 66.9 jit_solution(2224544159889598659)
XLA Ops:
  0.0 66.1 %gather_project_attend.1 = bf16[512,512]{1,0:T(8,128)(2,1)S(1)} custom-call(bf16[512,512]{1,0:T(8,128)(2,1)} %tok.1, bf16[2048,512]{1,0:T(8,128)(2,1)} %wq.1, bf16[2048,512]{1,0:T(8,128)(2,1)} %wk.1, bf16[2048,512]{1,0:T(8,128)(2,1)} %wv.1, s32[768]{0:T(1024)} %win.1, s32[2,768]{1,0:T(2,128)} %bitcast.1, s32[2,98304]{1,0:T(2,128)} %fb.1), custom_call_target="tpu_custom_call" | custom-call | flops 8999999488 | bytes 8000000 | tf_op jit(solution)/shard_map/gather_project_attend/pallas_call | solution.py:279
  66.1 0.8 %copy.9 = bf16[512,512]{1,0:T(8,128)(2,1)} copy(bf16[512,512]{1,0:T(8,128)(2,1)S(1)} %gather_project_attend.1) | data formatting | bytes 1048576

commit v5 on v4

--- a/solution.py
+++ b/solution.py
@@ -18,7 +18,8 @@
 SUBS = 4
 SUB = HALF // SUBS
 BND = 8
-OTHER = 10
+TMP = 10
+OTHER = 11
 LONG = 5
 SCALE = HEAD_DIM ** -0.5 * 1.4426950408889634
 LOW = -1e30
@@ -48,7 +49,7 @@
     mate = at(group, y, 1 - core)
     next_group = lax.rem(group + sgn + groups, groups)
     last_group = lax.rem(group - sgn + groups, groups)
-    side = at(next_group, y, core)
+    side, back_side = at(next_group, y, core), at(last_group, y, core)
 
     own_first = pl.multiple_of(seq * ROWS, ROWS)
     mine = pl.ds(pl.multiple_of(core * FEAT, FEAT), FEAT)
@@ -61,7 +62,7 @@
     ]
 
     barrier = pltpu.get_barrier_semaphore()
-    peers = (ahead, behind, mate, side, at(last_group, y, core))
+    peers = (ahead, behind, mate, side, back_side)
     for peer in peers:
         pl.semaphore_signal(barrier, inc=1, device_id=peer, device_id_type=MESH)
     load_tok.start()
@@ -102,19 +103,16 @@
         ref = big.at[slot, rows_of(half, k), theirs]
         pltpu.make_async_copy(ref, ref, recv_sem.at[slot + OTHER, half * SUBS + (k or 0)]).wait()
 
-    def step(s, pieces=range(SUBS)):
+    def step(s):
         f, b = slot_of(y - s * sgn), slot_of(y + s * sgn)
-        for k in pieces:
+        for k in range(SUBS):
             arrived(f, h_f, k)
-            if s < LONG:
-                send("ring", f, f, h_f, k, ahead)
+            send("ring", f, f, h_f, k, ahead)
+            arrived(b, h_b, k)
+            if s < LONG - 1:
+                send("ring", b, b, h_b, k, behind)
             else:
-                send("side", f, BND + 1, h_f, k, side)
-            arrived(b, h_b, k)
-            if s < LONG:
-                send("ring", b, b, h_b, k, behind)
-        if SUBS - 1 not in pieces:
-            return
+                send("side", b, TMP, h_b, k, back_side)
         if s == 1:
             send("side", f, BND, h_f, None, side)
         elif s in (3, 4):
@@ -124,18 +122,28 @@
         elif s != 2:
             to_mate(b, h_b)
 
-    def short_way(k):
-        f, b = slot_of(y - sgn), slot_of(y + sgn)
-        arrived(f, h_b, k)
-        send("side", f, BND, h_b, k, side)
-        arrived(b, h_f, k)
-        if k == SUBS - 1:
-            to_mate(b, h_f)
+    def pass_on(k):
+        arrived(TMP, h_b, k)
+        send("ring", TMP, BND + 1, h_b, k, behind)
+
+    def short_way():
+        for k in range(SUBS):
+            arrived(BND, h_b, k)
+            arrived(pair_near, h_f, k)
+        to_mate(BND, h_b)
+        to_mate(pair_near, h_f)
+
+    def last(k):
+        bnd_arrived(1, h_f, k)
+        arrived(pair_far, h_b, k)
+        to_mate(pair_far, h_b, k)
 
     def bnd_arrived(which, half, k=None):
         arrived(BND + which, half, k)
         to_mate(BND + which, half, k)
 
+    own_far = slot_of(y + 4)
+    pair_near, pair_far = slot_of(y + sgn), slot_of(y - 3 * sgn)
     g_near = half_id * 2
     g_far = 2 - g_near
 
@@ -192,8 +200,6 @@
             mean = acc[h, 0:HEAD_DIM, rows_of(half)] / acc[h, HEAD_DIM:HEAD_DIM + 1, rows_of(half)]
             out[rows_of(half), h * HEAD_DIM:(h + 1) * HEAD_DIM] = mean.T.astype(jnp.bfloat16)
 
-    own_far = slot_of(y + 4)
-    pair_near, pair_far = slot_of(y + sgn), slot_of(y - 3 * sgn)
     pair_run, bnd_run = 1 + sgn, 1 - sgn
     both, keyval = (0, 1), (1, 2)
 
@@ -202,6 +208,7 @@
         send("ring", y, y, h_b, k, behind, True)
     for half in both:
         to_mate(y, half, None, True)
+    send("side", y, TMP, h_f, None, back_side, True)
     for load in load_w:
         load.start()
     acc[...] = jnp.zeros_like(acc)
@@ -219,9 +226,10 @@
     mate_arrived(y, 1)
     first_part(part_own, y, g_near, 1, (0, 1, 2))
     step(3)
+    arrived(TMP, h_f)
     for k in range(SUBS):
         send("ring", y, y, h_b, k, ahead, True)
-        send("ring", y, y, h_f, k, behind, True)
+        send("ring", TMP, BND, h_f, k, behind)
     bnd_arrived(0, h_f)
     mate_arrived(pair_near, h_b)
     first_part(part_pair, pair_near, g_near, h_b, keyval)
@@ -230,38 +238,33 @@
     mate_arrived(pair_far, h_f)
     first_part(part_pair, pair_far, g_far, h_f, keyval)
     step(4)
-    short_way(0)
+    pass_on(0)
+    pass_on(1)
     mate_arrived(own_far, 0)
     second_part(part_own, own_far, g_far, 0, (0, 1, 2), 1)
-    short_way(1)
+    pass_on(2)
     bnd_arrived(1, h_b)
     mate_arrived(own_far, 1)
     second_part(part_own, own_far, g_far, 1, (0, 1, 2), 1)
-    short_way(2)
+    pass_on(3)
     attend(1, 0, ROWS, None, (0, 1))
-    short_way(3)
+    short_way()
     attend(1, 0, ROWS, None, (2, 3))
-    step(5, (0,))
     mate_arrived(BND + 1, h_b)
     first_part(part_bnd, BND + 1, g_near, h_b, keyval)
-    step(5, (1,))
-    for k in range(SUBS):
-        arrived(BND, h_b, k)
-    to_mate(BND, h_b)
+    last(0)
     mate_arrived(pair_near, h_f)
     second_part(part_pair, pair_near, g_near, h_f, keyval, pair_run)
-    step(5, (2,))
+    last(1)
     attend(pair_run, h_f * HALF, HALF)
-    step(5, (3,))
-    bnd_arrived(1, h_f, 0)
+    last(2)
     mate_arrived(BND, h_b)
     second_part(part_bnd, BND, g_far, h_b, keyval, bnd_run)
-    bnd_arrived(1, h_f, 1)
+    last(3)
     attend(bnd_run, h_b * HALF, HALF)
-    bnd_arrived(1, h_f, 2)
-    mate_arrived(pair_far, h_b)
+    for k in range(SUBS):
+        mate_arrived(pair_far, h_b, k)
     second_part(part_pair, pair_far, g_far, h_b, keyval, pair_run)
-    bnd_arrived(1, h_f, 3)
     attend(pair_run, h_b * HALF, HALF, h_b)
     finish(h_b)
     for k in range(SUBS):
@@ -282,7 +285,7 @@
         in_specs=[anywhere] * 4 + [scalars] * 2 + [anywhere],
         out_specs=pl.BlockSpec(memory_space=pltpu.VMEM),
         scratch_shapes=[
-            pltpu.VMEM((10, ROWS, 2 * FEAT), jnp.bfloat16),
+            pltpu.VMEM((11, ROWS, 2 * FEAT), jnp.bfloat16),
             pltpu.VMEM((2048, 3 * FEAT), jnp.bfloat16),
             pltpu.VMEM((ROWS, FEAT), jnp.bfloat16),
             pltpu.VMEM((3 * ROWS, FEAT), jnp.bfloat16),
@@ -296,7 +299,7 @@
             pltpu.VMEM((HEADS, 1, ROWS), jnp.float32),
             pltpu.SemaphoreType.DMA((12 * SUBS,)),
             pltpu.SemaphoreType.DMA((13 + 3 * SUBS,)),
-            pltpu.SemaphoreType.DMA((20, 2 * SUBS)),
+            pltpu.SemaphoreType.DMA((22, 2 * SUBS)),
             pltpu.SemaphoreType.DMA((5,)),
         ],
         compiler_params=pltpu.CompilerParams(

time: 67.1 us -> 64 us (0.954)
  Pallas kernels: 66.1 us -> 63 us
    pallas_call x1, Pallas kernels: 66.1 us -> 63 us  [local(): pl.pallas_call(functools.partial(kernel, groups), out_shape=pltpu.VMEM((R...]
where the time goes in v5:
time: 64 us; the launch traced here: 63.9 us
  Pallas kernels  63 us (98%)
  local copies, waits for them, and re-layouts  0.8 us (1%)
    pallas_call x1, Pallas kernels, local(): pl.pallas_call(functools.partial(kernel, groups), out_shape=pltpu.VMEM((R...  63 us

profile of v5, /device:TPU:1, one launch (start us, length us, event | category | flops | bytes accessed | tf_op | source)
XLA Modules:
  0.0 63.9 jit_solution(5918583039258057959)
XLA Ops:
  0.0 63.0 %gather_project_attend.1 = bf16[512,512]{1,0:T(8,128)(2,1)S(1)} custom-call(bf16[512,512]{1,0:T(8,128)(2,1)} %tok.1, bf16[2048,512]{1,0:T(8,128)(2,1)} %wq.1, bf16[2048,512]{1,0:T(8,128)(2,1)} %wk.1, bf16[2048,512]{1,0:T(8,128)(2,1)} %wv.1, s32[768]{0:T(1024)} %win.1, s32[2,768]{1,0:T(2,128)} %bitcast.1, s32[2,98304]{1,0:T(2,128)} %fb.1), custom_call_target="tpu_custom_call" | custom-call | flops 8999999488 | bytes 8000000 | tf_op jit(solution)/shard_map/gather_project_attend/pallas_call | solution.py:282
  63.1 0.8 %copy.9 = bf16[512,512]{1,0:T(8,128)(2,1)} copy(bf16[512,512]{1,0:T(8,128)(2,1)S(1)} %gather_project_attend.1) | data formatting | bytes 1048576

commit v6 on v5

--- a/solution.py
+++ b/solution.py
@@ -197,7 +197,7 @@
 
     def finish(half):
         for h in range(HEADS):
-            mean = acc[h, 0:HEAD_DIM, rows_of(half)] / acc[h, HEAD_DIM:HEAD_DIM + 1, rows_of(half)]
+            mean = acc[h, 0:HEAD_DIM, rows_of(half)] * (1.0 / acc[h, HEAD_DIM:HEAD_DIM + 1, rows_of(half)])
             out[rows_of(half), h * HEAD_DIM:(h + 1) * HEAD_DIM] = mean.T.astype(jnp.bfloat16)
 
     pair_run, bnd_run = 1 + sgn, 1 - sgn
@@ -247,9 +247,8 @@
     mate_arrived(own_far, 1)
     second_part(part_own, own_far, g_far, 1, (0, 1, 2), 1)
     pass_on(3)
-    attend(1, 0, ROWS, None, (0, 1))
+    attend(1, 0, ROWS)
     short_way()
-    attend(1, 0, ROWS, None, (2, 3))
     mate_arrived(BND + 1, h_b)
     first_part(part_bnd, BND + 1, g_near, h_b, keyval)
     last(0)
@@ -260,8 +259,9 @@
     last(2)
     mate_arrived(BND, h_b)
     second_part(part_bnd, BND, g_far, h_b, keyval, bnd_run)
+    attend(bnd_run, h_b * HALF, HALF, None, (0, 1))
     last(3)
-    attend(bnd_run, h_b * HALF, HALF)
+    attend(bnd_run, h_b * HALF, HALF, None, (2, 3))
     for k in range(SUBS):
         mate_arrived(pair_far, h_b, k)
     second_part(part_pair, pair_far, g_far, h_b, keyval, pair_run)

time: 64 us -> 65 us (1.016)
  Pallas kernels: 63 us -> 64 us
    pallas_call x1, Pallas kernels: 63 us -> 64 us  [local(): pl.pallas_call(functools.partial(kernel, groups), out_shape=pltpu.VMEM((R...]
where the time goes in v6:
time: 65 us; the launch traced here: 64.8 us
  Pallas kernels  64 us (98%)
  local copies, waits for them, and re-layouts  0.8 us (1%)
    pallas_call x1, Pallas kernels, local(): pl.pallas_call(functools.partial(kernel, groups), out_shape=pltpu.VMEM((R...  64 us

profile of v6, /device:TPU:1, one launch (start us, length us, event | category | flops | bytes accessed | tf_op | source)
XLA Modules:
  0.0 64.8 jit_solution(16458160206411114779)
XLA Ops:
  0.0 64.0 %gather_project_attend.1 = bf16[512,512]{1,0:T(8,128)(2,1)S(1)} custom-call(bf16[512,512]{1,0:T(8,128)(2,1)} %tok.1, bf16[2048,512]{1,0:T(8,128)(2,1)} %wq.1, bf16[2048,512]{1,0:T(8,128)(2,1)} %wk.1, bf16[2048,512]{1,0:T(8,128)(2,1)} %wv.1, s32[768]{0:T(1024)} %win.1, s32[2,768]{1,0:T(2,128)} %bitcast.1, s32[2,98304]{1,0:T(2,128)} %fb.1), custom_call_target="tpu_custom_call" | custom-call | flops 8999999488 | bytes 8000000 | tf_op jit(solution)/shard_map/gather_project_attend/pallas_call | solution.py:282
  64.0 0.8 %copy.9 = bf16[512,512]{1,0:T(8,128)(2,1)} copy(bf16[512,512]{1,0:T(8,128)(2,1)S(1)} %gather_project_attend.1) | data formatting | bytes 1048576
